TPU v7x, 32 devices: a whole 2x2x4 slice. The times are simulated.
32 devices in a mesh: grp: 2 (over y), sp: 4 (over z), flt: 2 (over x), rep: 2 (over core).
Axes of the slice: x: 2, y: 2, z: 4, core: 2. Of those that a mesh axis runs over, the one named last changes fastest.
Arguments:
- acts: float32 [64, 8, 8, 512], P(None, ('grp', 'sp'), ('flt', 'rep')), parts along dimension 1, may hold values from -6 to 6
- grad_out: float32 [64, 8, 8, 512], P(None, ('grp', 'sp'), ('flt', 'rep')), parts along dimension 1, may hold values from -6 to 6
- kernel: float32 [3, 3, 3, 64, 64], replicated, may hold values from -0.15625 to 0.15625
Outputs:
- input_grad: float32 [64, 8, 8, 512], P(None, ('grp', 'sp'), ('flt', 'rep')), parts along dimension 1
- weight_grad: float32 [6, 3, 3, 64, 64], P('grp'), parts along dimension 0
There are 2 independent parts, one for each index of `grp`. A program takes and returns all parts, laid end to end along the dimension named above; an argument that names none is the same for every part. Nothing has to cross between parts.
All inputs are finite; a program needn't handle non-finite values.
Results may differ from a plain program's by a relative error of at most 0.00007.
Values sent between devices are 32-bit elements; how exact they have to be, the bound alone decides.
A program may use at most 64 MiB of HBM per device.

v0:
```python
import math
import jax
import jax.numpy as jnp
from jax import lax
from jax.sharding import PartitionSpec as P


def padded_2(value, sides, width):
    for axis, dim in sides:
        count, length = (lax.axis_size(axis), value.shape[dim])
        up = [(i, (i + 1) % count) for i in range(count - 1)]
        down = [(j, i) for i, j in up]
        last = lax.slice_in_dim(value, length - width, length, axis=dim)
        first = lax.slice_in_dim(value, 0, width, axis=dim)
        before = lax.ppermute(last, axis, up)
        after = lax.ppermute(first, axis, down)
        value = jnp.concatenate([before, value, after], axis=dim)
    return value


def take_next(values):
    edge = jnp.zeros(values.shape[:-1] + (1,), values.dtype)
    return jnp.concatenate([values[..., 1:], edge], axis=-1)


def take_prior(values):
    edge = jnp.zeros(values.shape[:-1] + (1,), values.dtype)
    return jnp.concatenate([edge, values[..., :-1]], axis=-1)


def contract_last(left, right):
    return lax.dot_general(left, right, (((1,), (1,)), ((), ())), precision=lax.Precision.HIGHEST)


def per_device(acts, grad_out, kernel):
    cin = acts.shape[0]
    planes = acts.shape[1]
    rows = acts.shape[2]
    width = acts.shape[3]
    cout = grad_out.shape[0]
    voxels = (
        planes * lax.axis_size("sp") * rows * lax.axis_size("flt") * lax.axis_size("rep") * width
    )
    factor = 1.0 / math.sqrt(voxels)
    padded = padded_2(grad_out, (("sp", 1), (("flt", "rep"), 2)), 1)
    weights_tap = kernel.reshape(9, 3 * cin, cout)
    weight_terms = [jnp.zeros((3 * cin, cout), jnp.float32) for index in range(9)]
    source = acts[:, 0]
    source_stack = jnp.concatenate([take_prior(source), source, take_next(source)], axis=0).reshape(
        3 * cin, rows * width
    )
    partial_sum = jnp.zeros((3 * cin, rows * width), jnp.float32)
    for a_tap in range(3):
        for b_tap in range(3):
            index = 3 * a_tap + b_tap
            slab = padded[:, 2 - a_tap, 2 - b_tap : 2 - b_tap + rows, :].reshape(cout, rows * width)
            partial_sum = partial_sum + jnp.dot(
                weights_tap[index], slab, precision=lax.Precision.HIGHEST
            )
            weight_terms[index] = contract_last(source_stack, slab)
    parts_x = partial_sum.reshape(3, cin, rows, width)
    plane_out = take_next(parts_x[0]) + parts_x[1] + take_prior(parts_x[2])
    outputs = [plane_out]
    term = jnp.stack(weight_terms, axis=0).reshape(3, 3, 3, cin, cout) * factor
    weight_grad = lax.psum(term, ("sp", "flt", "rep"))
    input_grad = jnp.stack(outputs, axis=1)
    return (input_grad, weight_grad)


def solution(mesh):
    placed = (
        P(None, ("grp", "sp"), ("flt", "rep"), None),
        P(None, ("grp", "sp"), ("flt", "rep"), None),
        P(),
    )
    return jax.shard_map(
        per_device,
        mesh=mesh,
        in_specs=placed,
        out_specs=(P(None, ("grp", "sp"), ("flt", "rep"), None), P("grp", None, None, None, None)),
        check_vma=False,
    )
```

profile of v0, /device:TPU:0, one launch (start us, length us, event | category | flops | bytes accessed | tf_op | source)
XLA Modules:
  0.0 147.4 jit_solution(15860099137105820920)
XLA Ops:
  7.2 1.0 copy.11
  8.2 5.1 %collective-permute-start = (f32[64,1,2,512]{3,0,2,1:T(8,128)S(1)}, f32[64,1,2,512]{3,0,2,1:T(8,128)S(1)}, u32[]{:S(2)}, u32[]{:S(2)}) collective-permute-start(f32[64,1,2,512]{3,0,2,1:T(8,128)S(1)} %copy.11), channel_id=1, source_target_pairs={{0,4},{4,8},{8,12},{1,5},{5,9},{9,13},{2,6},{6,10},{10,14},{3,7},{... | collective-permute-start | bytes 786440 | tf_op jit(solution)/shard_map/ppermute | solution.py:15
  13.3 1.3 collective-permute-start.1
  14.6 4.2 %collective-permute-done = f32[64,1,2,512]{3,0,2,1:T(8,128)S(1)} collective-permute-done((f32[64,1,2,512]{3,0,2,1:T(8,128)S(1)}, f32[64,1,2,512]{3,0,2,1:T(8,128)S(1)}, u32[]{:S(2)}, u32[]{:S(2)}) %collective-permute-start) | collective-permute-done | bytes 262176 | tf_op jit(solution)/shard_map/ppermute | solution.py:15
  18.9 4.0 %collective-permute-done.1 = f32[64,1,2,512]{3,0,2,1:T(8,128)S(1)} collective-permute-done((f32[64,1,2,512]{3,0,2,1:T(8,128)S(1)}, f32[64,1,2,512]{3,0,2,1:T(8,128)S(1)}, u32[]{:S(2)}, u32[]{:S(2)}) %collective-permute-start.1) | collective-permute-done | bytes 262176 | tf_op jit(solution)/shard_map/ppermute | solution.py:16
  23.0 0.1 fusion.15
  23.1 1.3 collective-permute-start.2
  24.4 3.1 %collective-permute-start.3 = (f32[64,3,1,512]{3,0,2,1:T(8,128)S(1)}, f32[64,3,1,512]{3,0,2,1:T(8,128)S(1)}, u32[]{:S(2)}, u32[]{:S(2)}) collective-permute-start(f32[64,3,1,512]{3,0,2,1:T(8,128)S(1)} %get-tuple-element.14), channel_id=1, source_target_pairs={{0,1},{1,2},{2,3},{4,5},{5,6},{6,7},{8,9},{9,10},{10,11},{12,13},{... | collective-permute-start | bytes 1179656 | tf_op jit(solution)/shard_map/ppermute | solution.py:15
  27.5 0.3 fusion.16
  27.8 0.3 concatenate.41
  28.2 0.1 concatenate.44
  28.5 0.2 copy.15
  28.8 0.2 copy.20
  29.1 0.1 pad_maximum_fusion
  29.2 0.2 copy.14
  29.5 0.2 copy.16
  29.8 0.2 copy.17
  30.0 0.2 copy.18
  30.3 0.2 copy.19
  30.6 0.2 copy.21
  30.9 0.9 fusion.13
  31.7 0.9 fusion.12
  32.6 0.9 fusion.11
  33.5 0.9 fusion.10
  34.4 0.9 fusion.9
  35.2 0.9 fusion.8
  36.1 0.9 fusion.7
  37.0 0.9 fusion.6
  37.9 0.9 fusion.5
  38.8 1.2 copy.22
  40.1 1.1 copy-done.2
  41.2 0.8 convolution_bitcast_fusion.5
  42.0 0.8 convolution_add_fusion.2
  42.8 0.8 fusion.4
  43.5 0.8 fusion.3
  44.3 0.9 convolution_add_fusion.1
  45.3 0.8 fusion.2
  46.0 0.8 fusion.1
  46.8 0.8 convolution_add_fusion
  47.6 0.8 fusion
  48.4 0.1 fusion.14
  48.4 0.2 squeeze.48
  48.6 0.3 slice.117
  49.0 0.2 squeeze.50
  49.2 0.2 squeeze.49
  49.4 1.0 add_bitcast_fusion
  50.5 87.9 %all-reduce.6.cloned.1.call-done = f32[3,3,3,64,64]{4,3,2,1,0:T(8,128)} async-done(((f32[3,3,3,64,64]{4,3,2,1,0:T(8,128)}), f32[3,3,3,64,64]{4,3,2,1,0:T(8,128)}) %all-reduce.6.cloned.1.call-update) | async-done | bytes 442384 | tf_op jit(solution)/shard_map/psum | solution.py:65
  138.4 2.2 %copy.49 = f32[3,3,3,64,64]{4,3,2,1,0:T(8,128)} copy(f32[3,3,3,64,64]{4,3,2,1,0:T(8,128)} %all-reduce.6.cloned.1.call-done) | data formatting | bytes 884736
  (28 shorter events, 0.9 us)
Async XLA Ops:
  7.2 131.2 %all-reduce.6.cloned.1.call-start = ((), (), s32[]{:S(2)}) async-start(), calls=%async_computation | async-start | bytes 1769472 | tf_op jit(solution)/shard_map/psum | solution.py:65
  8.2 10.6 %copy-start.1 = (f32[64,1,2,512]{3,2,1,0:T(2,128)S(1)}, f32[64,1,2,512]{3,2,1,0:T(2,128)}, u32[]{:S(2)}) copy-start(f32[64,1,2,512]{3,2,1,0:T(2,128)} %param.4) | copy-start | bytes 786436
  8.2 10.6 %collective-permute-start = (f32[64,1,2,512]{3,0,2,1:T(8,128)S(1)}, f32[64,1,2,512]{3,0,2,1:T(8,128)S(1)}, u32[]{:S(2)}, u32[]{:S(2)}) collective-permute-start(f32[64,1,2,512]{3,0,2,1:T(8,128)S(1)} %copy.11), channel_id=1, source_target_pairs={{0,4},{4,8},{8,12},{1,5},{5,9},{9,13},{2,6},{6,10},{10,14},{3,7},{... | collective-permute-start | bytes 786440 | tf_op jit(solution)/shard_map/ppermute | solution.py:15
  13.3 9.7 %collective-permute-start.1 = (f32[64,1,2,512]{3,0,2,1:T(8,128)S(1)}, f32[64,1,2,512]{3,0,2,1:T(8,128)S(1)}, u32[]{:S(2)}, u32[]{:S(2)}) collective-permute-start(f32[64,1,2,512]{3,0,2,1:T(8,128)S(1)} %copy.11), channel_id=1, source_target_pairs={{4,0},{8,4},{12,8},{5,1},{9,5},{13,9},{6,2},{10,6},{14,10},{7,3},{... | collective-permute-start | bytes 786440 | tf_op jit(solution)/shard_map/ppermute | solution.py:16
  23.0 4.5 %copy-start = (f32[64,1,2,512]{3,2,1,0:T(2,128)S(1)}, f32[64,1,2,512]{3,2,1,0:T(2,128)}, u32[]{:S(2)}) copy-start(f32[64,1,2,512]{3,2,1,0:T(2,128)} %param.3) | copy-start | bytes 786436
  23.1 6.0 %collective-permute-start.2 = (f32[64,3,1,512]{3,0,2,1:T(8,128)S(1)}, f32[64,3,1,512]{3,0,2,1:T(8,128)S(1)}, u32[]{:S(2)}, u32[]{:S(2)}) collective-permute-start(f32[64,3,1,512]{3,0,2,1:T(8,128)S(1)} %get-tuple-element.15), channel_id=1, source_target_pairs={{1,0},{2,1},{3,2},{5,4},{6,5},{7,6},{9,8},{10,9},{11,10},{13,12},{... | collective-permute-start | bytes 1179656 | tf_op jit(solution)/shard_map/ppermute | solution.py:16
  24.4 4.7 %collective-permute-start.3 = (f32[64,3,1,512]{3,0,2,1:T(8,128)S(1)}, f32[64,3,1,512]{3,0,2,1:T(8,128)S(1)}, u32[]{:S(2)}, u32[]{:S(2)}) collective-permute-start(f32[64,3,1,512]{3,0,2,1:T(8,128)S(1)} %get-tuple-element.14), channel_id=1, source_target_pairs={{0,1},{1,2},{2,3},{4,5},{5,6},{6,7},{8,9},{9,10},{10,11},{12,13},{... | collective-permute-start | bytes 1179656 | tf_op jit(solution)/shard_map/ppermute | solution.py:15
  40.0 1.2 copy-start.2
Sparse Core Ops, SparseCore 0:
  40.2 98.1 all-reduce.5
where the time goes:
time: 148 us; the launch traced here: 147 us
  waiting for transfers between devices  96.2 us (65%)
  matrix products  15 us (10%)
  between operations  14.4 us (10%)
  starting transfers between devices  10.8 us (7%)
  local copies, waits for them, and re-layouts  9.81 us (7%)
    psum x1, waiting for transfers between devices, per_device(): weight_grad = lax.psum(term, ('sp', 'flt', 'rep'))  87.9 us
    ppermute x2, starting transfers between devices, padded_2(): before = lax.ppermute(last, axis, up)  8.13 us
    dot_general x9, matrix products, contract_last(): lax.dot_general(left, right, (((1,), (1,)), ((), ())), precision=lax.Prec...  7.91 us
    dot_general x9, matrix products, per_device(): jnp.dot(weights_tap[index], slab, precision=lax.Precision.HIGHEST)  7.09 us
    unnamed x24, local copies, waits for them, and re-layouts  5.03 us
    ppermute x2, waiting for transfers between devices, padded_2(): before = lax.ppermute(last, axis, up)  4.23 us
    ppermute x2, waiting for transfers between devices, padded_2(): after = lax.ppermute(first, axis, down)  4.05 us
  transfers between devices with their start and end apart: 5, of which 3 were waited for; matrix products, arithmetic and copies ran while one was open for 7% of the time, Pallas kernels for 0%

commit v1 on v0

--- a/solution.py
+++ b/solution.py
@@ -62,7 +62,7 @@
     plane_out = take_next(parts_x[0]) + parts_x[1] + take_prior(parts_x[2])
     outputs = [plane_out]
     term = jnp.stack(weight_terms, axis=0).reshape(3, 3, 3, cin, cout) * factor
-    weight_grad = lax.psum(term, ("sp", "flt", "rep"))
+    weight_grad = lax.psum(lax.psum(term, ("flt", "rep")), "sp")
     input_grad = jnp.stack(outputs, axis=1)
     return (input_grad, weight_grad)
 

time: 148 us -> 139 us (0.939)
  waiting for transfers between devices: 96.2 us -> 87.8 us
    psum x1 -> x2, waiting for transfers between devices: 87.9 us -> 79.5 us  [per_device(): weight_grad = lax.psum(lax.psum(term, ('flt', 'rep')), 'sp')]
  transfers between devices with their start and end apart: 5 -> 6, of which waited for: 3 -> 4; matrix products, arithmetic and copies ran while one was open for 7% -> 8% of each run, Pallas kernels for 0% -> 0%
where the time goes in v1:
time: 139 us
  waiting for transfers between devices  87.8 us (63%)
  matrix products  14.9 us (11%)
  between operations  14.4 us (10%)
  starting transfers between devices  11 us (8%)
  local copies, waits for them, and re-layouts  9.59 us (7%)
    psum x2, waiting for transfers between devices, per_device(): weight_grad = lax.psum(lax.psum(term, ('flt', 'rep')), 'sp')  79.5 us
    ppermute x2, starting transfers between devices, padded_2(): before = lax.ppermute(last, axis, up)  8.13 us
    dot_general x9, matrix products, contract_last(): lax.dot_general(left, right, (((1,), (1,)), ((), ())), precision=lax.Prec...  7.91 us
    dot_general x9, matrix products, per_device(): jnp.dot(weights_tap[index], slab, precision=lax.Precision.HIGHEST)  6.98 us
    unnamed x24, local copies, waits for them, and re-layouts  4.8 us
    ppermute x2, waiting for transfers between devices, padded_2(): before = lax.ppermute(last, axis, up)  4.23 us
    ppermute x2, waiting for transfers between devices, padded_2(): after = lax.ppermute(first, axis, down)  4.05 us
  transfers between devices with their start and end apart: 6, of which 4 were waited for; matrix products, arithmetic and copies ran while one was open for 8% of the time, Pallas kernels for 0%

profile of v1, /device:TPU:0, one launch (start us, length us, event | category | flops | bytes accessed | tf_op | source)
XLA Modules:
  0.0 138.9 jit_solution(12874821826051982028)
XLA Ops:
  7.2 1.0 copy.11
  8.2 5.1 %collective-permute-start = (f32[64,1,2,512]{3,0,2,1:T(8,128)S(1)}, f32[64,1,2,512]{3,0,2,1:T(8,128)S(1)}, u32[]{:S(2)}, u32[]{:S(2)}) collective-permute-start(f32[64,1,2,512]{3,0,2,1:T(8,128)S(1)} %copy.11), channel_id=1, source_target_pairs={{0,4},{4,8},{8,12},{1,5},{5,9},{9,13},{2,6},{6,10},{10,14},{3,7},{... | collective-permute-start | bytes 786440 | tf_op jit(solution)/shard_map/ppermute | solution.py:15
  13.3 1.3 collective-permute-start.1
  14.6 4.2 %collective-permute-done = f32[64,1,2,512]{3,0,2,1:T(8,128)S(1)} collective-permute-done((f32[64,1,2,512]{3,0,2,1:T(8,128)S(1)}, f32[64,1,2,512]{3,0,2,1:T(8,128)S(1)}, u32[]{:S(2)}, u32[]{:S(2)}) %collective-permute-start) | collective-permute-done | bytes 262176 | tf_op jit(solution)/shard_map/ppermute | solution.py:15
  18.9 4.0 %collective-permute-done.1 = f32[64,1,2,512]{3,0,2,1:T(8,128)S(1)} collective-permute-done((f32[64,1,2,512]{3,0,2,1:T(8,128)S(1)}, f32[64,1,2,512]{3,0,2,1:T(8,128)S(1)}, u32[]{:S(2)}, u32[]{:S(2)}) %collective-permute-start.1) | collective-permute-done | bytes 262176 | tf_op jit(solution)/shard_map/ppermute | solution.py:16
  23.1 1.3 collective-permute-start.2
  24.4 3.1 %collective-permute-start.3 = (f32[64,3,1,512]{3,0,2,1:T(8,128)S(1)}, f32[64,3,1,512]{3,0,2,1:T(8,128)S(1)}, u32[]{:S(2)}, u32[]{:S(2)}) collective-permute-start(f32[64,3,1,512]{3,0,2,1:T(8,128)S(1)} %get-tuple-element.14), channel_id=1, source_target_pairs={{0,1},{1,2},{2,3},{4,5},{5,6},{6,7},{8,9},{9,10},{10,11},{12,13},{... | collective-permute-start | bytes 1179656 | tf_op jit(solution)/shard_map/ppermute | solution.py:15
  27.5 0.3 fusion.16
  27.8 0.3 concatenate.41
  28.2 0.1 concatenate.44
  28.5 0.2 copy.15
  28.8 0.2 copy.20
  29.1 0.1 pad_maximum_fusion
  29.2 0.2 copy.14
  29.5 0.2 copy.16
  29.8 0.2 copy.17
  30.0 0.2 copy.18
  30.3 0.2 copy.19
  30.6 0.2 copy.21
  30.9 0.9 fusion.13
  31.7 0.9 fusion.12
  32.6 0.9 fusion.11
  33.5 0.9 fusion.10
  34.4 0.9 fusion.9
  35.2 0.9 fusion.8
  36.1 0.9 fusion.7
  37.0 0.9 fusion.6
  37.9 0.9 fusion.5
  38.8 1.2 copy.22
  40.1 0.2 all-reduce.9.cloned.1.call-start
  40.3 0.9 copy-done.2
  41.2 0.8 convolution_bitcast_fusion.5
  42.0 0.8 convolution_add_fusion.2
  42.8 0.8 fusion.4
  43.5 0.8 fusion.3
  44.3 0.8 convolution_add_fusion.1
  45.1 0.8 fusion.2
  45.9 0.8 fusion.1
  46.7 0.8 convolution_add_fusion
  47.5 0.8 fusion
  48.3 32.3 %all-reduce.7.cloned.1.call-done = f32[3,3,3,64,64]{4,3,2,1,0:T(8,128)} async-done(((f32[3,3,3,64,64]{4,3,2,1,0:T(8,128)}), f32[3,3,3,64,64]{4,3,2,1,0:T(8,128)}) %all-reduce.7.cloned.1.call-update) | async-done | bytes 442384 | tf_op jit(solution)/shard_map/psum | solution.py:65
  80.6 0.2 squeeze.48
  80.9 0.3 slice.117
  81.2 0.2 squeeze.50
  81.4 0.2 squeeze.49
  81.6 1.0 add_bitcast_fusion
  82.7 47.2 %all-reduce.9.cloned.1.call-done = f32[3,3,3,64,64]{4,3,2,1,0:T(8,128)} async-done(((f32[3,3,3,64,64]{4,3,2,1,0:T(8,128)}), f32[3,3,3,64,64]{4,3,2,1,0:T(8,128)}) %all-reduce.9.cloned.1.call-update) | async-done | bytes 442384 | tf_op jit(solution)/shard_map/psum | solution.py:65
  129.9 2.2 %copy.50 = f32[3,3,3,64,64]{4,3,2,1,0:T(8,128)} copy(f32[3,3,3,64,64]{4,3,2,1,0:T(8,128)} %all-reduce.9.cloned.1.call-done) | data formatting | bytes 884736
  (31 shorter events, 1.0 us)
Async XLA Ops:
  7.2 73.4 %all-reduce.7.cloned.1.call-start = ((), (), s32[]{:S(2)}) async-start(), calls=%async_computation | async-start | bytes 1769472 | tf_op jit(solution)/shard_map/psum | solution.py:65
  8.2 10.6 %copy-start.1 = (f32[64,1,2,512]{3,2,1,0:T(2,128)S(1)}, f32[64,1,2,512]{3,2,1,0:T(2,128)}, u32[]{:S(2)}) copy-start(f32[64,1,2,512]{3,2,1,0:T(2,128)} %param.4) | copy-start | bytes 786436
  8.2 10.6 %collective-permute-start = (f32[64,1,2,512]{3,0,2,1:T(8,128)S(1)}, f32[64,1,2,512]{3,0,2,1:T(8,128)S(1)}, u32[]{:S(2)}, u32[]{:S(2)}) collective-permute-start(f32[64,1,2,512]{3,0,2,1:T(8,128)S(1)} %copy.11), channel_id=1, source_target_pairs={{0,4},{4,8},{8,12},{1,5},{5,9},{9,13},{2,6},{6,10},{10,14},{3,7},{... | collective-permute-start | bytes 786440 | tf_op jit(solution)/shard_map/ppermute | solution.py:15
  13.3 9.7 %collective-permute-start.1 = (f32[64,1,2,512]{3,0,2,1:T(8,128)S(1)}, f32[64,1,2,512]{3,0,2,1:T(8,128)S(1)}, u32[]{:S(2)}, u32[]{:S(2)}) collective-permute-start(f32[64,1,2,512]{3,0,2,1:T(8,128)S(1)} %copy.11), channel_id=1, source_target_pairs={{4,0},{8,4},{12,8},{5,1},{9,5},{13,9},{6,2},{10,6},{14,10},{7,3},{... | collective-permute-start | bytes 786440 | tf_op jit(solution)/shard_map/ppermute | solution.py:16
  23.0 4.5 %copy-start = (f32[64,1,2,512]{3,2,1,0:T(2,128)S(1)}, f32[64,1,2,512]{3,2,1,0:T(2,128)}, u32[]{:S(2)}) copy-start(f32[64,1,2,512]{3,2,1,0:T(2,128)} %param.3) | copy-start | bytes 786436
  23.1 6.0 %collective-permute-start.2 = (f32[64,3,1,512]{3,0,2,1:T(8,128)S(1)}, f32[64,3,1,512]{3,0,2,1:T(8,128)S(1)}, u32[]{:S(2)}, u32[]{:S(2)}) collective-permute-start(f32[64,3,1,512]{3,0,2,1:T(8,128)S(1)} %get-tuple-element.15), channel_id=1, source_target_pairs={{1,0},{2,1},{3,2},{5,4},{6,5},{7,6},{9,8},{10,9},{11,10},{13,12},{... | collective-permute-start | bytes 1179656 | tf_op jit(solution)/shard_map/ppermute | solution.py:16
  24.4 4.7 %collective-permute-start.3 = (f32[64,3,1,512]{3,0,2,1:T(8,128)S(1)}, f32[64,3,1,512]{3,0,2,1:T(8,128)S(1)}, u32[]{:S(2)}, u32[]{:S(2)}) collective-permute-start(f32[64,3,1,512]{3,0,2,1:T(8,128)S(1)} %get-tuple-element.14), channel_id=1, source_target_pairs={{0,1},{1,2},{2,3},{4,5},{5,6},{6,7},{8,9},{9,10},{10,11},{12,13},{... | collective-permute-start | bytes 1179656 | tf_op jit(solution)/shard_map/ppermute | solution.py:15
  40.0 1.2 copy-start.2
  40.1 89.8 %all-reduce.9.cloned.1.call-start = ((), (), s32[]{:S(2)}) async-start(), calls=%async_computation.1 | async-start | bytes 1769472 | tf_op jit(solution)/shard_map/psum | solution.py:65
Sparse Core Ops, SparseCore 0:
  40.2 40.3 all-reduce.6
  82.9 46.9 all-reduce.8
